TPU v7x, 32 devices: a whole 2x2x4 slice. The times are simulated.
32 devices in a mesh: parts: 2 (over y), pre: 4 (over z), tp: 4 (over x, core).
Axes of the slice: x: 2, y: 2, z: 4, core: 2. Of those that a mesh axis runs over, the one named last changes fastest.
Arguments:
- queries: bfloat16 [4096, 4096], P(('parts', 'pre'), 'tp'), parts along dimension 0, may hold values from -4.5 to 4.5
- new_keys: bfloat16 [4096, 1024], P(('parts', 'pre'), 'tp'), parts along dimension 0, may hold values from -4.5 to 4.5
- new_values: bfloat16 [4096, 1024], P(('parts', 'pre'), 'tp'), parts along dimension 0, may hold values from -4 to 4
- lengths: int32 [8], P('parts'), parts along dimension 0, may hold values from 1 to 1024, 2048 in all
- block_slot: int32 [256], P('parts'), parts along dimension 0, may hold values from 0 to 127, as said below
Outputs:
- attended: bfloat16 [4096, 4096], P(('parts', 'pre'), 'tp'), parts along dimension 0
- kv_cache: bfloat16 [256, 16, 2048], P(('parts', 'pre'), None, 'tp'), parts along dimension 0
There are 2 independent parts, one for each index of `parts`. A program takes and returns all parts, laid end to end along the dimension named above; each array names one. Nothing has to cross between parts.
Inputs may be any that keep to these rules, and one draw needn't show every extreme that they name: `block_slot`: A permutation of the 128 slots. The 32 blocks held by one index of pre (blocks of its own rows) take exactly 8 slots of every decode owner.
All inputs are finite; a program needn't handle non-finite values.
Results may differ from a plain program's by a relative error of at most 0.0036.
Values may be sent and summed in bfloat16 or wider, within the bound.
No kernel may reach another device: no remote copies, remote signals or barrier semaphores. Data moves between devices by JAX's collectives and lax.ppermute only.
A program may use at most 64 MiB of HBM per device.

v0:
```python
import functools
import math

import jax
import jax.numpy as jnp
from jax import lax
from jax.experimental import pallas as pl
from jax.experimental.pallas import tpu as pltpu
from jax.sharding import PartitionSpec as P

HD = 128
BLK = 16
GROUP = 4
TILE = 256
MASKED = -1e30
EXP_SCALE = math.log2(math.e) * HD ** (-0.5)

VMEM = pl.BlockSpec(memory_space=pltpu.VMEM)
SMEM = pl.BlockSpec(memory_space=pltpu.SMEM)
HBM = pl.BlockSpec(memory_space=pltpu.HBM)


def start_of(lengths_ref, position):
    end = jnp.int32(0)
    start = jnp.int32(0)
    for r in range(lengths_ref.shape[0]):
        end = end + lengths_ref[r]
        start = jnp.where(end <= position, end, start)
    return start


def row_starts(lengths_ref, positions):
    end = jnp.int32(0)
    starts = jnp.zeros_like(positions)
    for r in range(lengths_ref.shape[0]):
        end = end + lengths_ref[r]
        starts = jnp.where(positions >= end, end, starts)
    return starts


def fill_bias(bias_ref, lengths_ref, row_first, key_first, low, high, causal):
    shape = (high - low, TILE)
    positions = row_first + lax.broadcasted_iota(jnp.int32, (8, TILE), 1)
    starts = row_starts(lengths_ref, positions)
    keys = key_first + low + lax.broadcasted_iota(jnp.int32, shape, 0)
    keys = keys.reshape((high - low) // 8, 8, TILE)
    allowed = keys >= starts[None]
    if causal:
        allowed = allowed & (keys <= positions[None])
    bias_ref[low:high] = jnp.where(allowed, 0.0, MASKED).reshape(shape)


def turn_values(v_ref, turned):
    for g in range(turned.shape[0]):
        turned[g] = v_ref[:, g * HD : (g + 1) * HD].T


def lanes_of(tile, j):
    return slice((tile * GROUP + j) * TILE, (tile * GROUP + j + 1) * TILE)


def weigh(q_ref, k_ref, bias_ref, old_top, tile, low, high, g, emit):
    keys = k_ref[low:high, g * HD : (g + 1) * HD]
    heads = range(g * GROUP, (g + 1) * GROUP)
    queries = jnp.concatenate(
        [q_ref[tile * TILE : (tile + 1) * TILE, h * HD : (h + 1) * HD] for h in heads], axis=0
    )
    all_scores = lax.dot_general(
        keys, queries, (((1,), (1,)), ((), ())), preferred_element_type=jnp.float32
    )
    for j in range(GROUP):
        scores = all_scores[:, j * TILE : (j + 1) * TILE] + bias_ref[low:high]
        scores = scores.reshape((high - low) // 8, 8, TILE)
        highest = jnp.max(jnp.max(scores, axis=0), axis=0, keepdims=True)
        top = jnp.broadcast_to(highest, (8, TILE))
        factor = None
        if old_top is not None:
            old = old_top[g, :, lanes_of(tile, j)]
            top = jnp.maximum(old, top)
            factor = jnp.exp2((old - top) * EXP_SCALE)
        weights = jnp.exp2((scores - top[None]) * EXP_SCALE)
        total = jnp.sum(weights, axis=0)
        emit(j, weights.reshape(high - low, TILE).astype(jnp.bfloat16), top, factor, total)


def mix(values, weights, g, tile, old, emit):
    all_added = jnp.dot(values, weights, preferred_element_type=jnp.float32)
    for j in range(GROUP):
        at = lanes_of(tile, j)
        value = all_added[:, j * TILE : (j + 1) * TILE]
        if old is not None:
            acc_ref, factor_ref = old
            factor = factor_ref[g, :, at]
            kept = acc_ref[g, :, at].reshape(HD // 8, 8, TILE) * factor[None]
            value = value + kept.reshape(HD, TILE)
        emit(g, j, value)


def keep(acc_ref, tile):
    def emit(g, j, value):
        acc_ref[g, :, lanes_of(tile, j)] = value

    return emit


def finish(out_ref, row):
    def emit(g, j, value, totals):
        head = g * GROUP + j
        total = jnp.broadcast_to(jnp.sum(totals, axis=0, keepdims=True), totals.shape)
        value = value.reshape(HD // 8, 8, TILE) * (1.0 / total)[None]
        value = value.reshape(HD, TILE).astype(out_ref.dtype).T
        out_ref[row : row + TILE, head * HD : (head + 1) * HD] = value

    return emit


def block_of(k_ref, v_ref, row):
    parts = []
    for g in range(k_ref.shape[1] // HD):
        span = slice(g * HD, (g + 1) * HD)
        parts += [k_ref[pl.ds(row, BLK), span], v_ref[pl.ds(row, BLK), span]]
    return jnp.concatenate(parts, axis=1)


def own_slot(slot, me, blocks):
    local = slot - me * blocks
    return jnp.where((local >= 0) & (local < blocks), local, blocks)


def list_places(places_ref, slot_ref, hops, pre, blocks):
    me = lax.axis_index("pre")
    stride = blocks // pre + 1
    for distance in range(2, pre):
        source = lax.rem(me - distance + pre, pre)

        def step(b, n):
            at = own_slot(slot_ref[source * blocks + b], me, blocks)
            places_ref[(distance - 2) * stride + n] = at
            if distance <= hops:
                places_ref[(pre - 2 + distance - 2) * stride + n] = b
            return n + jnp.where(at < blocks, 1, 0)

        lax.fori_loop(0, blocks, step, jnp.int32(0), unroll=8)


def own_kernel(
    pre, hops, lengths_ref, slot_ref, q_hbm, k_hbm, v_hbm,
    q_ref, acc_ref, sum_ref, top_ref, cache_ref, places_ref, *refs,
):
    sent_hbm, refs = refs[: pre - 2], refs[pre - 2 :]
    k_ref, v_ref, turned, bias, sent_values, sent, counts, sems, load_sems = refs
    loads = [
        pltpu.make_async_copy(src, dst, load_sems.at[n])
        for n, (src, dst) in enumerate(((k_hbm, k_ref), (v_hbm, v_ref), (q_hbm, q_ref)))
    ]
    for load in loads:
        load.start()
    rows = q_ref.shape[0]
    blocks = rows // BLK
    per_peer = blocks // pre
    me = lax.axis_index("pre")
    first = me * rows
    for owner in range(pre):
        counts[owner] = 0
    list_places(places_ref, slot_ref, hops, pre, blocks)
    loads[0].wait()
    loads[1].wait()

    def step(b, _):
        slot = slot_ref[me * blocks + b]
        owner = slot // blocks
        n = counts[owner]
        counts[owner] = n + 1
        distance = lax.rem(owner - me + pre, pre)
        row = pl.multiple_of(b * BLK, BLK)
        on_ring = (distance > 1) & (distance <= hops)
        at = jnp.where(on_ring, (distance - 2) * per_peer + n, (hops - 1) * per_peer)
        sent_values[at] = v_ref[pl.ds(row, BLK)]
        beyond = (distance - hops - 1) * per_peer + n
        at = jnp.where(distance > hops, beyond, (pre - 1 - hops) * per_peer)
        block = block_of(k_ref, v_ref, row)
        sent[at] = block
        cache_ref[own_slot(slot, me, blocks)] = block
        return 0

    lax.fori_loop(0, blocks, step, 0, unroll=4)
    packed = [sent_values.at[n * per_peer : (n + 1) * per_peer] for n in range(hops - 1)]
    packed += [sent.at[n * per_peer : (n + 1) * per_peer] for n in range(pre - 1 - hops)]
    stores = [
        pltpu.make_async_copy(src, dst, sems.at[n])
        for n, (src, dst) in enumerate(zip(packed, sent_hbm))
    ]
    for store in stores:
        store.start()
    turn_values(v_ref, turned)
    loads[2].wait()
    for tile in range(rows // TILE):
        high = (tile + 1) * TILE
        fill_bias(bias, lengths_ref, first + tile * TILE, first, 0, high, True)
        for g in range(turned.shape[0]):
            all_weights = []

            def emit(j, weights, top, factor, total):
                all_weights.append(weights)
                top_ref[g, :, lanes_of(tile, j)] = top
                sum_ref[g, :, lanes_of(tile, j)] = total

            weigh(q_ref, k_ref, bias, None, tile, 0, high, g, emit)
            all_weights = jnp.concatenate(all_weights, axis=1)
            mix(turned[g, :, :high], all_weights, g, tile, None, keep(acc_ref, tile))
    for store in stores:
        store.wait()


def lowest_key(lengths_ref, hop, tile, rows):
    first = lax.axis_index("pre") * rows
    key_first = first - hop * rows
    low = jnp.maximum(start_of(lengths_ref, first + tile * TILE) - key_first, 0)
    return jnp.where(key_first >= 0, jnp.minimum(low, rows), rows)


def where_seen(low, rows, act):
    for at in range(0, rows, TILE):
        pl.when((low >= at) & (low < at + TILE))(functools.partial(act, at))


def scores_kernel(hop, lengths_ref, q_ref, k_ref, old_top, old_sum, weights_ref, factor_ref, sum_ref, *refs):
    *top_refs, bias = refs
    rows = q_ref.shape[0]
    first = lax.axis_index("pre") * rows
    for tile in range(rows // TILE):

        def act(at):
            fill_bias(
                bias, lengths_ref, first + tile * TILE, first - hop * rows, at, rows, False
            )
            for g in range(weights_ref.shape[1]):

                def emit(j, weights, top, factor, total):
                    lanes = lanes_of(tile, j)
                    sum_ref[g, :, lanes] = old_sum[g, :, lanes] * factor + total
                    weights_ref[tile, g, at:rows, j * TILE : (j + 1) * TILE] = weights
                    for top_ref in top_refs:
                        top_ref[g, :, lanes_of(tile, j)] = top
                    factor_ref[g, :, lanes_of(tile, j)] = factor

                weigh(q_ref, k_ref, bias, old_top, tile, at, rows, g, emit)

        where_seen(lowest_key(lengths_ref, hop, tile, rows), rows, act)


def place_blocks(cache, slot_ref, k_ref, v_ref, distance, pre, blocks):
    me = lax.axis_index("pre")
    source = lax.rem(me - distance + pre, pre)

    def step(b, _):
        at = own_slot(slot_ref[source * blocks + b], me, blocks)
        cache[at] = block_of(k_ref, v_ref, pl.multiple_of(b * BLK, BLK))
        return 0

    lax.fori_loop(0, blocks, step, 0, unroll=8)


def place_listed(cache, places_ref, hop, pre, k_ref, v_ref, got_ref):
    me = lax.axis_index("pre")
    per_peer = got_ref.shape[0]
    stride = per_peer + 1

    def place(values_at):
        for n in range(per_peer):
            at = places_ref[(hop - 2) * stride + n]
            b = places_ref[(pre - 2 + hop - 2) * stride + n]
            rows = pl.ds(pl.multiple_of(b * BLK, BLK), BLK)
            values = values_at(n, rows)
            parts = []
            for g in range(k_ref.shape[1] // HD):
                span = slice(g * HD, (g + 1) * HD)
                parts += [k_ref[rows, span], values[:, span]]
            cache[at] = jnp.concatenate(parts, axis=1)

    pl.when(me >= hop - 1)(lambda: place(lambda n, rows: v_ref[rows]))
    pl.when(me < hop - 1)(lambda: place(lambda n, rows: got_ref[n]))


def place_packed(cache, places_ref, distance, got_ref):
    per_peer = got_ref.shape[0]
    for n in range(per_peer):
        cache[places_ref[(distance - 2) * (per_peer + 1) + n]] = got_ref[n]


def values_kernel(
    hop, hops, pre, lengths_ref, slot_ref, v_ref, k_ref, weights_ref, factor_ref,
    acc_in, sum_in, old_sum, cache_in, *refs,
):
    first_out, last = hop == 1, hop == hops
    refs = list(refs)
    if not first_out:
        refs.pop(0)
    got_ref = None if first_out else refs.pop(0)
    got_far = [refs.pop(0) for _ in range(hops + 1, pre)] if last else []
    out_hbm, cache_out = refs.pop(0), refs.pop(0)
    acc_ref = None if last else refs.pop(0)
    turned, out_buf, sems, *rest = refs
    rows = v_ref.shape[0]
    blocks = rows // BLK
    tiles = rows // TILE
    kv_count = turned.shape[0]

    cache = rest[0] if last else cache_out
    cache[...] = cache_in[...]
    if first_out:
        place_blocks(cache, slot_ref, k_ref, v_ref, hop, pre, blocks)
    else:
        place_listed(cache, slot_ref, hop, pre, k_ref, v_ref, got_ref)
    if last:
        for n, far_ref in enumerate(got_far):
            place_packed(cache, slot_ref, hops + 1 + n, far_ref)
        cache_store = pltpu.make_async_copy(cache.at[0:blocks], cache_out, sems.at[tiles])
        cache_store.start()

    lows = [lowest_key(lengths_ref, hop, tile, rows) for tile in range(tiles)]
    pl.when(lows[0] < rows)(functools.partial(turn_values, v_ref, turned))
    stores = []
    for tile, low in enumerate(lows):
        end_it = finish(out_buf, tile * TILE)

        def act(at):
            def emit(g, j, value):
                if not last:
                    keep(acc_ref, tile)(g, j, value)
                end_it(g, j, value, sum_in[g, :, lanes_of(tile, j)])

            for g in range(kv_count):
                weights = weights_ref[tile, g, at:rows]
                old = (acc_in, factor_ref)
                mix(turned[g, :, at:rows], weights, g, tile, old, emit)

        where_seen(low, rows, act)
        span = slice(tile * TILE, (tile + 1) * TILE)
        store = pltpu.make_async_copy(out_buf.at[span], out_hbm.at[span], sems.at[tile])
        stores.append(store)
        if first_out:

            @pl.when(low == rows)
            def _():
                for g in range(kv_count):
                    for j in range(GROUP):
                        end_it(g, j, *(ref[g, :, lanes_of(tile, j)] for ref in (acc_in, old_sum)))

            store.start()
        else:
            pl.when(low < rows)(store.start)
    for low, store in zip(lows, stores):
        if first_out:
            store.wait()
        else:
            pl.when(low < rows)(store.wait)
    if last:
        cache_store.wait()


def on_device(queries, new_keys, new_values, lengths, block_slot):
    rows, q_width = queries.shape
    kv_width = new_keys.shape[1]
    kv_count = kv_width // HD
    blocks = rows // BLK
    pre = lax.axis_size("pre")
    per_peer = blocks // pre
    hops = pre // 2
    tiles = rows // TILE
    bf16, f32 = jnp.bfloat16, jnp.float32
    shape = jax.ShapeDtypeStruct
    params = pltpu.CompilerParams(vmem_limit_bytes=24 * 2**20)
    own_params = pltpu.CompilerParams(vmem_limit_bytes=44 * 2**20)
    ring = [(i, (i + 1) % pre) for i in range(pre)]
    acc_shape = shape((kv_count, HD, GROUP * rows), f32)
    stat_shape = shape((kv_count, 8, GROUP * rows), f32)
    weights_shape = shape((tiles, kv_count, rows, GROUP * TILE), bf16)
    attended_shape = shape(queries.shape, bf16)
    cache_shape = shape((blocks, BLK, 2 * kv_width), bf16)
    open_cache = shape((blocks + 1, BLK, 2 * kv_width), bf16)
    turned = pltpu.VMEM((kv_count, HD, rows), bf16)
    bias = pltpu.VMEM((rows, TILE), f32)

    def cost(share, moved):
        pairs = int(rows * rows * share)
        return pl.CostEstimate(
            flops=4 * pairs * q_width,
            bytes_accessed=moved * 2**20,
            transcendentals=pairs * kv_count * GROUP,
        )

    def after(array, *others):
        return lax.optimization_barrier((array, *others))[0]

    k, v = lax.ppermute(new_keys, "pre", ring), lax.ppermute(new_values, "pre", ring)

    packed = (shape((per_peer, BLK, kv_width), bf16),) * (hops - 1)
    packed += (shape((per_peer, BLK, 2 * kv_width), bf16),) * (pre - 1 - hops)
    places = shape(((pre - 2 + hops - 1) * (per_peer + 1),), jnp.int32)
    in_hbm = (
        pltpu.with_memory_space_constraint(x, pltpu.HBM) for x in (queries, new_keys, new_values)
    )
    q, acc, total, top, cache, places, *sent = pl.pallas_call(
        functools.partial(own_kernel, pre, hops),
        out_shape=(attended_shape, acc_shape, stat_shape, stat_shape, open_cache, places)
        + packed,
        in_specs=[SMEM, SMEM] + [HBM] * 3,
        out_specs=(VMEM,) * 5 + (SMEM,) + (HBM,) * (pre - 2),
        scratch_shapes=[
            pltpu.VMEM((rows, kv_width), bf16),
            pltpu.VMEM((rows, kv_width), bf16),
            turned,
            bias,
            pltpu.VMEM(((hops - 1) * per_peer + 1, BLK, kv_width), bf16),
            pltpu.VMEM(((pre - 1 - hops) * per_peer + 1, BLK, 2 * kv_width), bf16),
            pltpu.SMEM((pre,), jnp.int32),
            pltpu.SemaphoreType.DMA((pre - 2,)),
            pltpu.SemaphoreType.DMA((3,)),
        ],
        cost_estimate=cost(1, 4),
        compiler_params=own_params,
        name="own_attention",
    )(lengths, block_slot, *in_hbm)
    got = []
    k = after(k, top)
    attended = None
    for hop in range(1, hops + 1):
        first_out, last = hop == 1, hop == hops
        onward = [(i, i + 1) for i in range(hop - 1, pre - 1)]
        next_k = None if last else lax.ppermute(k, "pre", ring)
        weights, factor, new_total, *tops = pl.pallas_call(
            functools.partial(scores_kernel, hop),
            out_shape=(weights_shape, stat_shape, stat_shape) + (() if last else (stat_shape,)),
            in_specs=[SMEM] + [VMEM] * 4,
            out_specs=(VMEM,) * (3 if last else 4),
            scratch_shapes=[bias],
            cost_estimate=cost(0.5, 3),
            compiler_params=params,
            name="scores",
        )(lengths, q, k, top, total)
        v = after(v, factor)
        next_v = None if last else lax.ppermute(v, "pre", onward)
        if first_out:
            for d in range(2, pre):
                targets = range(d - 1 if d <= hops else pre)
                pairs = [((i - d) % pre, i) for i in targets]
                got.append(lax.ppermute(after(sent[d - 2], v), "pre", pairs))
        carry = () if last else (acc_shape,)
        extra = [] if first_out else [attended]
        extra += [] if first_out else [got[hop - 2]]
        extra += got[hops - 1 :] if last else []
        attended, cache, *state = pl.pallas_call(
            functools.partial(values_kernel, hop, hops, pre),
            out_shape=(attended_shape, cache_shape if last else open_cache)
            + carry,
            in_specs=[SMEM, SMEM]
            + [VMEM] * 8
            + ([] if first_out else [HBM])
            + [VMEM] * (len(extra) - 1),
            out_specs=(HBM, HBM if last else VMEM)
            + (VMEM,) * len(carry),
            scratch_shapes=[
                turned,
                pltpu.VMEM((rows, q_width), bf16),
                pltpu.SemaphoreType.DMA((tiles + 1,)),
            ]
            + ([pltpu.VMEM(open_cache.shape, bf16)] if last else []),
            input_output_aliases={} if first_out else {10: 0},
            cost_estimate=cost(0.5, 3),
            compiler_params=params,
            name="values",
        )(lengths, block_slot if first_out else places, v, k, weights, factor, acc, new_total, total, cache, *extra)
        if not last:
            (top,) = tops
            (acc,) = state
            total = new_total
            k, v = after(next_k, total), next_v

    return (attended, cache)


def solution(mesh):
    placed = (
        P(("parts", "pre"), "tp"),
        P(("parts", "pre"), "tp"),
        P(("parts", "pre"), "tp"),
        P("parts"),
        P("parts"),
    )
    return jax.shard_map(
        on_device,
        mesh=mesh,
        in_specs=placed,
        out_specs=(P(("parts", "pre"), "tp"), P(("parts", "pre"), None, "tp")),
        check_vma=False,
    )
```

profile of v0, /device:TPU:0, one launch (start us, length us, event | category | flops | bytes accessed | tf_op | source)
XLA Modules:
  0.0 30.8 jit_solution(13250632601957002995)
XLA Ops:
  0.6 3.1 %collective-permute-start.1 = (bf16[512,256]{1,0:T(8,128)(2,1)}, bf16[512,256]{1,0:T(8,128)(2,1)S(1)}, u32[]{:S(2)}, u32[]{:S(2)}) collective-permute-start(bf16[512,256]{1,0:T(8,128)(2,1)} %k_hbm.1), channel_id=1, source_target_pairs={{0,4},{4,8},{8,12},{12,0},{1,5},{5,9},{9,13},{13,1},{2,6},{6,10},{... | collective-permute-start | bytes 786440 | tf_op jit(solution)/shard_map/ppermute | solution.py:396
  3.7 1.6 %collective-permute-start = (bf16[512,256]{1,0:T(8,128)(2,1)}, bf16[512,256]{1,0:T(8,128)(2,1)S(1)}, u32[]{:S(2)}, u32[]{:S(2)}) collective-permute-start(bf16[512,256]{1,0:T(8,128)(2,1)} %v_hbm.1), channel_id=1, source_target_pairs={{0,4},{4,8},{8,12},{12,0},{1,5},{5,9},{9,13},{13,1},{2,6},{6,10},{... | collective-permute-start | bytes 786440 | tf_op jit(solution)/shard_map/ppermute | solution.py:396
  5.3 0.0 copy-start
  5.3 0.7 %copy-done = s32[4]{0:T(128)S(1)} copy-done((s32[4]{0:T(128)S(1)}, s32[4]{0:T(128)}, u32[]{:S(2)}) %copy-start) | copy-done | bytes 40
  5.9 0.0 copy-start.1
  5.9 0.7 %copy-done.1 = s32[128]{0:T(128)S(1)} copy-done((s32[128]{0:T(128)S(1)}, s32[128]{0:T(128)}, u32[]{:S(2)}) %copy-start.1) | copy-done | bytes 536
  6.6 5.9 %own_attention.1 = (bf16[512,1024]{1,0:T(8,128)(2,1)S(1)}, f32[2,128,2048]{2,1,0:T(8,128)S(1)}, f32[2,8,2048]{2,1,0:T(8,128)S(1)}, f32[2,8,2048]{2,1,0:T(8,128)S...) custom-call(s32[4]{0:T(128)S(1)} %copy-done, ...), custom_call_target="tpu_custom_call" | custom-call | flops 1073741824 | bytes 4194304 | tf_op jit(solution)/shard_map/own_attention/pallas_call | solution.py:404
  12.5 0.5 %collective-permute-done.1.k_ref = bf16[512,256]{1,0:T(8,128)(2,1)S(1)} collective-permute-done((bf16[512,256]{1,0:T(8,128)(2,1)}, bf16[512,256]{1,0:T(8,128)(2,1)S(1)}, u32[]{:S(2)}, u32[]{:S(2)}) %collective-permute-start.1) | collective-permute-done | bytes 262176 | tf_op jit(solution)/shard_map/ppermute | solution.py:396
  13.1 1.1 %collective-permute-start.3 = (bf16[512,256]{1,0:T(8,128)(2,1)S(1)}, bf16[512,256]{1,0:T(8,128)(2,1)S(1)}, u32[]{:S(2)}, u32[]{:S(2)}) collective-permute-start(bf16[512,256]{1,0:T(8,128)(2,1)S(1)} %collective-permute-done.1.k_ref), channel_id=1, source_target_pairs={{0,4},{4,8},{8,12},{12,0},{1,5},{5,9},{9,13},{13,1},{2,6},{6,10},{... | collective-permute-start | bytes 786440 | tf_op jit(solution)/shard_map/ppermute | solution.py:431
  14.2 0.6 %scores.2 = (bf16[2,2,512,1024]{3,2,1,0:T(8,128)(2,1)S(1)}, f32[2,8,2048]{2,1,0:T(8,128)S(1)}, f32[2,8,2048]{2,1,0:T(8,128)S(1)}, f32[2,8,2048]{2,1,0:T(8,128)S(1)}) custom-call(s32[4]{0:T(128)S(1)} %copy-done, bf16[512,1024]{1,0:T(8,128)(2,1)S(1)} %get-tuple-element.27.q_ref, bf16[512,256]{1,0:T(8,128)(2,1)S(1)} %collective-permute-done.1.k_ref, ...), custom_call_target="tpu_custom_call" | custom-call | flops 536870912 | bytes 3145728 | tf_op jit(solution)/shard_map/scores/pallas_call | solution.py:432
  14.8 3.9 %collective-permute-done.v_ref = bf16[512,256]{1,0:T(8,128)(2,1)S(1)} collective-permute-done((bf16[512,256]{1,0:T(8,128)(2,1)}, bf16[512,256]{1,0:T(8,128)(2,1)S(1)}, u32[]{:S(2)}, u32[]{:S(2)}) %collective-permute-start) | collective-permute-done | bytes 262176 | tf_op jit(solution)/shard_map/ppermute | solution.py:396
  18.7 1.9 %collective-permute-start.2 = (bf16[512,256]{1,0:T(8,128)(2,1)S(1)}, bf16[512,256]{1,0:T(8,128)(2,1)S(1)}, u32[]{:S(2)}, u32[]{:S(2)}) collective-permute-start(bf16[512,256]{1,0:T(8,128)(2,1)S(1)} %collective-permute-done.v_ref), channel_id=1, source_target_pairs={{0,4},{4,8},{8,12},{1,5},{5,9},{9,13},{2,6},{6,10},{10,14},{3,7},{... | collective-permute-start | bytes 786440 | tf_op jit(solution)/shard_map/ppermute | solution.py:443
  20.6 1.4 %collective-permute-start.5 = (bf16[8,16,512]{2,1,0:T(8,128)(2,1)S(1)}, bf16[8,16,512]{2,1,0:T(8,128)(2,1)S(1)}, u32[]{:S(2)}, u32[]{:S(2)}) collective-permute-start(bf16[8,16,512]{2,1,0:T(8,128)(2,1)S(1)} %get-tuple-element.49), channel_id=1, source_target_pairs={{4,0},{8,4},{12,8},{0,12},{5,1},{9,5},{13,9},{1,13},{6,2},{10,6},{... | collective-permute-start | bytes 393224 | tf_op jit(solution)/shard_map/ppermute | solution.py:448
  22.1 1.3 %collective-permute-start.4 = (bf16[8,16,256]{2,1,0:T(8,128)(2,1)S(1)}, bf16[8,16,256]{2,1,0:T(8,128)(2,1)S(1)}, u32[]{:S(2)}, u32[]{:S(2)}) collective-permute-start(bf16[8,16,256]{2,1,0:T(8,128)(2,1)S(1)} %get-tuple-element.47), channel_id=1, source_target_pairs={{8,0},{9,1},{10,2},{11,3},{24,16},{25,17},{26,18},{27,19}} | collective-permute-start | bytes 196616 | tf_op jit(solution)/shard_map/ppermute | solution.py:448
  23.4 2.1 %values.2 = (bf16[512,1024]{1,0:T(8,128)(2,1)}, bf16[33,16,512]{2,1,0:T(8,128)(2,1)S(1)}, f32[2,128,2048]{2,1,0:T(8,128)S(1)}) custom-call(s32[4]{0:T(128)S(1)} %copy-done, s32[128]{0:T(128)S(1)} %copy-done.1, bf16[512,256]{1,0:T(8,128)(2,1)S(1)} %collective-permute-done.v_ref, bf16[512,256]{1,0:T(8,128)(2,1)S(1)} %collective-permute-done.1.k_ref, ...), custom_call_target="tpu_custom_call" | custom-call | flops 536870912 | bytes 3145728 | tf_op jit(solution)/shard_map/values/pallas_call | solution.py:453
  25.5 0.0 collective-permute-done.3.k_ref
  25.5 0.8 %scores.3 = (bf16[2,2,512,1024]{3,2,1,0:T(8,128)(2,1)S(1)}, f32[2,8,2048]{2,1,0:T(8,128)S(1)}, f32[2,8,2048]{2,1,0:T(8,128)S(1)}) custom-call(s32[4]{0:T(128)S(1)} %copy-done, bf16[512,1024]{1,0:T(8,128)(2,1)S(1)} %get-tuple-element.27.q_ref, bf16[512,256]{1,0:T(8,128)(2,1)S(1)} %collective-permute-done.3.k_ref, ...), custom_call_target="tpu_custom_call" | custom-call | flops 536870912 | bytes 3145728 | tf_op jit(solution)/shard_map/scores/pallas_call | solution.py:432
  26.2 1.2 %collective-permute-done.2.v_ref = bf16[512,256]{1,0:T(8,128)(2,1)S(1)} collective-permute-done((bf16[512,256]{1,0:T(8,128)(2,1)S(1)}, bf16[512,256]{1,0:T(8,128)(2,1)S(1)}, u32[]{:S(2)}, u32[]{:S(2)}) %collective-permute-start.2) | collective-permute-done | bytes 262176 | tf_op jit(solution)/shard_map/ppermute | solution.py:443
  27.5 1.7 %collective-permute-done.4.refs_1_ = bf16[8,16,256]{2,1,0:T(8,128)(2,1)S(1)} collective-permute-done((bf16[8,16,256]{2,1,0:T(8,128)(2,1)S(1)}, bf16[8,16,256]{2,1,0:T(8,128)(2,1)S(1)}, u32[]{:S(2)}, u32[]{:S(2)}) %collective-permute-start.4) | collective-permute-done | bytes 65568 | tf_op jit(solution)/shard_map/ppermute | solution.py:448
  29.1 0.0 collective-permute-done.5.refs_2_
  29.2 1.4 %values.3 = (bf16[512,1024]{1,0:T(8,128)(2,1)}, bf16[32,16,512]{2,1,0:T(8,128)(2,1)}) custom-call(s32[4]{0:T(128)S(1)} %copy-done, s32[27]{0:T(128)S(1)} %get-tuple-element.26.slot_ref, bf16[512,256]{1,0:T(8,128)(2,1)S(1)} %collective-permute-done.2.v_ref, bf16[512,256]{1,0:T(8,128)(2,1)S(1)} %collective-permute-done.3.k_ref, ...), custom_call_target="tpu_custom_call", output_to_operand_aliasing={{0}: (10, {})} | custom-call | flops 536870912 | bytes 3145728 | tf_op jit(solution)/shard_map/values/pallas_call | solution.py:453
Async XLA Ops:
  0.6 12.4 %collective-permute-start.1 = (bf16[512,256]{1,0:T(8,128)(2,1)}, bf16[512,256]{1,0:T(8,128)(2,1)S(1)}, u32[]{:S(2)}, u32[]{:S(2)}) collective-permute-start(bf16[512,256]{1,0:T(8,128)(2,1)} %k_hbm.1), channel_id=1, source_target_pairs={{0,4},{4,8},{8,12},{12,0},{1,5},{5,9},{9,13},{13,1},{2,6},{6,10},{... | collective-permute-start | bytes 786440 | tf_op jit(solution)/shard_map/ppermute | solution.py:396
  3.7 15.0 %collective-permute-start = (bf16[512,256]{1,0:T(8,128)(2,1)}, bf16[512,256]{1,0:T(8,128)(2,1)S(1)}, u32[]{:S(2)}, u32[]{:S(2)}) collective-permute-start(bf16[512,256]{1,0:T(8,128)(2,1)} %v_hbm.1), channel_id=1, source_target_pairs={{0,4},{4,8},{8,12},{12,0},{1,5},{5,9},{9,13},{13,1},{2,6},{6,10},{... | collective-permute-start | bytes 786440 | tf_op jit(solution)/shard_map/ppermute | solution.py:396
  5.3 0.7 %copy-start = (s32[4]{0:T(128)S(1)}, s32[4]{0:T(128)}, u32[]{:S(2)}) copy-start(s32[4]{0:T(128)} %lengths_ref.9) | copy-start | bytes 52
  5.9 0.7 %copy-start.1 = (s32[128]{0:T(128)S(1)}, s32[128]{0:T(128)}, u32[]{:S(2)}) copy-start(s32[128]{0:T(128)} %slot_ref.3) | copy-start | bytes 1540
  13.1 12.4 %collective-permute-start.3 = (bf16[512,256]{1,0:T(8,128)(2,1)S(1)}, bf16[512,256]{1,0:T(8,128)(2,1)S(1)}, u32[]{:S(2)}, u32[]{:S(2)}) collective-permute-start(bf16[512,256]{1,0:T(8,128)(2,1)S(1)} %collective-permute-done.1.k_ref), channel_id=1, source_target_pairs={{0,4},{4,8},{8,12},{12,0},{1,5},{5,9},{9,13},{13,1},{2,6},{6,10},{... | collective-permute-start | bytes 786440 | tf_op jit(solution)/shard_map/ppermute | solution.py:431
  18.7 8.8 %collective-permute-start.2 = (bf16[512,256]{1,0:T(8,128)(2,1)S(1)}, bf16[512,256]{1,0:T(8,128)(2,1)S(1)}, u32[]{:S(2)}, u32[]{:S(2)}) collective-permute-start(bf16[512,256]{1,0:T(8,128)(2,1)S(1)} %collective-permute-done.v_ref), channel_id=1, source_target_pairs={{0,4},{4,8},{8,12},{1,5},{5,9},{9,13},{2,6},{6,10},{10,14},{3,7},{... | collective-permute-start | bytes 786440 | tf_op jit(solution)/shard_map/ppermute | solution.py:443
  20.6 8.5 %collective-permute-start.5 = (bf16[8,16,512]{2,1,0:T(8,128)(2,1)S(1)}, bf16[8,16,512]{2,1,0:T(8,128)(2,1)S(1)}, u32[]{:S(2)}, u32[]{:S(2)}) collective-permute-start(bf16[8,16,512]{2,1,0:T(8,128)(2,1)S(1)} %get-tuple-element.49), channel_id=1, source_target_pairs={{4,0},{8,4},{12,8},{0,12},{5,1},{9,5},{13,9},{1,13},{6,2},{10,6},{... | collective-permute-start | bytes 393224 | tf_op jit(solution)/shard_map/ppermute | solution.py:448
  22.1 7.0 %collective-permute-start.4 = (bf16[8,16,256]{2,1,0:T(8,128)(2,1)S(1)}, bf16[8,16,256]{2,1,0:T(8,128)(2,1)S(1)}, u32[]{:S(2)}, u32[]{:S(2)}) collective-permute-start(bf16[8,16,256]{2,1,0:T(8,128)(2,1)S(1)} %get-tuple-element.47), channel_id=1, source_target_pairs={{8,0},{9,1},{10,2},{11,3},{24,16},{25,17},{26,18},{27,19}} | collective-permute-start | bytes 196616 | tf_op jit(solution)/shard_map/ppermute | solution.py:448
where the time goes:
time: 31.1 us; the launch traced here: 30.8 us
  Pallas kernels  10.8 us (35%)
  starting transfers between devices  10.4 us (33%)
  waiting for transfers between devices  7.4 us (24%)
  local copies, waits for them, and re-layouts  1.31 us (4%)
  between operations  0.85 us (3%)
    pallas_call x1, Pallas kernels, on_device(): pl.pallas_call(functools.partial(own_kernel, pre, hops), out_shape=(atten...  5.93 us
    ppermute x1, waiting for transfers between devices, on_device(): lax.ppermute(new_values, 'pre', ring)  3.91 us
    pallas_call x2, Pallas kernels, on_device(): pl.pallas_call(functools.partial(values_kernel, hop, hops, pre), out_shap...  3.5 us
    ppermute x1, starting transfers between devices, on_device(): lax.ppermute(new_keys, 'pre', ring)  3.08 us
    ppermute x2, starting transfers between devices, on_device(): got.append(lax.ppermute(after(sent[d - 2], v), 'pre', pairs))  2.73 us
    ppermute x1, starting transfers between devices, on_device(): next_v = None if last else lax.ppermute(v, 'pre', onward)  1.94 us
    ppermute x2, waiting for transfers between devices, on_device(): got.append(lax.ppermute(after(sent[d - 2], v), 'pre', pairs))  1.71 us
    ppermute x1, starting transfers between devices, on_device(): lax.ppermute(new_values, 'pre', ring)  1.58 us
  transfers between devices with their start and end apart: 6, of which 4 were waited for; matrix products, arithmetic and copies ran while one was open for 0% of the time, Pallas kernels for 30%

commit v1 on v0

--- a/solution.py
+++ b/solution.py
@@ -306,6 +306,38 @@
     tiles = rows // TILE
     kv_count = turned.shape[0]
 
+    lows = [lowest_key(lengths_ref, hop, tile, rows) for tile in range(tiles)]
+    pl.when(lows[0] < rows)(functools.partial(turn_values, v_ref, turned))
+    stores = []
+    for tile, low in enumerate(lows):
+        end_it = finish(out_buf, tile * TILE)
+
+        def act(at):
+            def emit(g, j, value):
+                if not last:
+                    keep(acc_ref, tile)(g, j, value)
+                end_it(g, j, value, sum_in[g, :, lanes_of(tile, j)])
+
+            for g in range(kv_count):
+                weights = weights_ref[tile, g, at:rows]
+                old = (acc_in, factor_ref)
+                mix(turned[g, :, at:rows], weights, g, tile, old, emit)
+
+        where_seen(low, rows, act)
+        span = slice(tile * TILE, (tile + 1) * TILE)
+        store = pltpu.make_async_copy(out_buf.at[span], out_hbm.at[span], sems.at[tile])
+        stores.append(store)
+        if first_out:
+
+            @pl.when(low == rows)
+            def _():
+                for g in range(kv_count):
+                    for j in range(GROUP):
+                        end_it(g, j, *(ref[g, :, lanes_of(tile, j)] for ref in (acc_in, old_sum)))
+
+            store.start()
+        else:
+            pl.when(low < rows)(store.start)
     cache = rest[0] if last else cache_out
     cache[...] = cache_in[...]
     if first_out:
@@ -318,38 +350,6 @@
         cache_store = pltpu.make_async_copy(cache.at[0:blocks], cache_out, sems.at[tiles])
         cache_store.start()
 
-    lows = [lowest_key(lengths_ref, hop, tile, rows) for tile in range(tiles)]
-    pl.when(lows[0] < rows)(functools.partial(turn_values, v_ref, turned))
-    stores = []
-    for tile, low in enumerate(lows):
-        end_it = finish(out_buf, tile * TILE)
-
-        def act(at):
-            def emit(g, j, value):
-                if not last:
-                    keep(acc_ref, tile)(g, j, value)
-                end_it(g, j, value, sum_in[g, :, lanes_of(tile, j)])
-
-            for g in range(kv_count):
-                weights = weights_ref[tile, g, at:rows]
-                old = (acc_in, factor_ref)
-                mix(turned[g, :, at:rows], weights, g, tile, old, emit)
-
-        where_seen(low, rows, act)
-        span = slice(tile * TILE, (tile + 1) * TILE)
-        store = pltpu.make_async_copy(out_buf.at[span], out_hbm.at[span], sems.at[tile])
-        stores.append(store)
-        if first_out:
-
-            @pl.when(low == rows)
-            def _():
-                for g in range(kv_count):
-                    for j in range(GROUP):
-                        end_it(g, j, *(ref[g, :, lanes_of(tile, j)] for ref in (acc_in, old_sum)))
-
-            store.start()
-        else:
-            pl.when(low < rows)(store.start)
     for low, store in zip(lows, stores):
         if first_out:
             store.wait()

time: 31.1 us -> 31.3 us (level)
  no operation moved by 1% of the time
where the time goes in v1:
time: 31.3 us; the launch traced here: 30.8 us
  Pallas kernels  10.6 us (34%)
  starting transfers between devices  10.4 us (33%)
  waiting for transfers between devices  7.61 us (24%)
  local copies, waits for them, and re-layouts  1.31 us (4%)
  between operations  0.85 us (3%)
    pallas_call x1, Pallas kernels, on_device(): pl.pallas_call(functools.partial(own_kernel, pre, hops), out_shape=(atten...  5.93 us
    ppermute x1, waiting for transfers between devices, on_device(): lax.ppermute(new_values, 'pre', ring)  3.91 us
    pallas_call x2, Pallas kernels, on_device(): pl.pallas_call(functools.partial(values_kernel, hop, hops, pre), out_shap...  3.33 us
    ppermute x1, starting transfers between devices, on_device(): lax.ppermute(new_keys, 'pre', ring)  3.08 us
    ppermute x2, starting transfers between devices, on_device(): got.append(lax.ppermute(after(sent[d - 2], v), 'pre', pairs))  2.73 us
    ppermute x1, starting transfers between devices, on_device(): next_v = None if last else lax.ppermute(v, 'pre', onward)  1.94 us
    ppermute x2, waiting for transfers between devices, on_device(): got.append(lax.ppermute(after(sent[d - 2], v), 'pre', pairs))  1.71 us
    ppermute x1, starting transfers between devices, on_device(): lax.ppermute(new_values, 'pre', ring)  1.58 us
  transfers between devices with their start and end apart: 6, of which 4 were waited for; matrix products, arithmetic and copies ran while one was open for 0% of the time, Pallas kernels for 30%

profile of v1, /device:TPU:0, one launch (start us, length us, event | category | flops | bytes accessed | tf_op | source)
XLA Modules:
  0.0 30.8 jit_solution(17299153812315331112)
XLA Ops:
  0.6 3.1 %collective-permute-start.1 = (bf16[512,256]{1,0:T(8,128)(2,1)}, bf16[512,256]{1,0:T(8,128)(2,1)S(1)}, u32[]{:S(2)}, u32[]{:S(2)}) collective-permute-start(bf16[512,256]{1,0:T(8,128)(2,1)} %k_hbm.1), channel_id=1, source_target_pairs={{0,4},{4,8},{8,12},{12,0},{1,5},{5,9},{9,13},{13,1},{2,6},{6,10},{... | collective-permute-start | bytes 786440 | tf_op jit(solution)/shard_map/ppermute | solution.py:396
  3.7 1.6 %collective-permute-start = (bf16[512,256]{1,0:T(8,128)(2,1)}, bf16[512,256]{1,0:T(8,128)(2,1)S(1)}, u32[]{:S(2)}, u32[]{:S(2)}) collective-permute-start(bf16[512,256]{1,0:T(8,128)(2,1)} %v_hbm.1), channel_id=1, source_target_pairs={{0,4},{4,8},{8,12},{12,0},{1,5},{5,9},{9,13},{13,1},{2,6},{6,10},{... | collective-permute-start | bytes 786440 | tf_op jit(solution)/shard_map/ppermute | solution.py:396
  5.3 0.0 copy-start
  5.3 0.7 %copy-done = s32[4]{0:T(128)S(1)} copy-done((s32[4]{0:T(128)S(1)}, s32[4]{0:T(128)}, u32[]{:S(2)}) %copy-start) | copy-done | bytes 40
  5.9 0.0 copy-start.1
  5.9 0.7 %copy-done.1 = s32[128]{0:T(128)S(1)} copy-done((s32[128]{0:T(128)S(1)}, s32[128]{0:T(128)}, u32[]{:S(2)}) %copy-start.1) | copy-done | bytes 536
  6.6 5.9 %own_attention.1 = (bf16[512,1024]{1,0:T(8,128)(2,1)S(1)}, f32[2,128,2048]{2,1,0:T(8,128)S(1)}, f32[2,8,2048]{2,1,0:T(8,128)S(1)}, f32[2,8,2048]{2,1,0:T(8,128)S...) custom-call(s32[4]{0:T(128)S(1)} %copy-done, ...), custom_call_target="tpu_custom_call" | custom-call | flops 1073741824 | bytes 4194304 | tf_op jit(solution)/shard_map/own_attention/pallas_call | solution.py:404
  12.5 0.5 %collective-permute-done.1.k_ref = bf16[512,256]{1,0:T(8,128)(2,1)S(1)} collective-permute-done((bf16[512,256]{1,0:T(8,128)(2,1)}, bf16[512,256]{1,0:T(8,128)(2,1)S(1)}, u32[]{:S(2)}, u32[]{:S(2)}) %collective-permute-start.1) | collective-permute-done | bytes 262176 | tf_op jit(solution)/shard_map/ppermute | solution.py:396
  13.1 1.1 %collective-permute-start.3 = (bf16[512,256]{1,0:T(8,128)(2,1)S(1)}, bf16[512,256]{1,0:T(8,128)(2,1)S(1)}, u32[]{:S(2)}, u32[]{:S(2)}) collective-permute-start(bf16[512,256]{1,0:T(8,128)(2,1)S(1)} %collective-permute-done.1.k_ref), channel_id=1, source_target_pairs={{0,4},{4,8},{8,12},{12,0},{1,5},{5,9},{9,13},{13,1},{2,6},{6,10},{... | collective-permute-start | bytes 786440 | tf_op jit(solution)/shard_map/ppermute | solution.py:431
  14.2 0.6 %scores.2 = (bf16[2,2,512,1024]{3,2,1,0:T(8,128)(2,1)S(1)}, f32[2,8,2048]{2,1,0:T(8,128)S(1)}, f32[2,8,2048]{2,1,0:T(8,128)S(1)}, f32[2,8,2048]{2,1,0:T(8,128)S(1)}) custom-call(s32[4]{0:T(128)S(1)} %copy-done, bf16[512,1024]{1,0:T(8,128)(2,1)S(1)} %get-tuple-element.27.q_ref, bf16[512,256]{1,0:T(8,128)(2,1)S(1)} %collective-permute-done.1.k_ref, ...), custom_call_target="tpu_custom_call" | custom-call | flops 536870912 | bytes 3145728 | tf_op jit(solution)/shard_map/scores/pallas_call | solution.py:432
  14.8 3.9 %collective-permute-done.v_ref = bf16[512,256]{1,0:T(8,128)(2,1)S(1)} collective-permute-done((bf16[512,256]{1,0:T(8,128)(2,1)}, bf16[512,256]{1,0:T(8,128)(2,1)S(1)}, u32[]{:S(2)}, u32[]{:S(2)}) %collective-permute-start) | collective-permute-done | bytes 262176 | tf_op jit(solution)/shard_map/ppermute | solution.py:396
  18.7 1.9 %collective-permute-start.2 = (bf16[512,256]{1,0:T(8,128)(2,1)S(1)}, bf16[512,256]{1,0:T(8,128)(2,1)S(1)}, u32[]{:S(2)}, u32[]{:S(2)}) collective-permute-start(bf16[512,256]{1,0:T(8,128)(2,1)S(1)} %collective-permute-done.v_ref), channel_id=1, source_target_pairs={{0,4},{4,8},{8,12},{1,5},{5,9},{9,13},{2,6},{6,10},{10,14},{3,7},{... | collective-permute-start | bytes 786440 | tf_op jit(solution)/shard_map/ppermute | solution.py:443
  20.6 1.4 %collective-permute-start.5 = (bf16[8,16,512]{2,1,0:T(8,128)(2,1)S(1)}, bf16[8,16,512]{2,1,0:T(8,128)(2,1)S(1)}, u32[]{:S(2)}, u32[]{:S(2)}) collective-permute-start(bf16[8,16,512]{2,1,0:T(8,128)(2,1)S(1)} %get-tuple-element.49), channel_id=1, source_target_pairs={{4,0},{8,4},{12,8},{0,12},{5,1},{9,5},{13,9},{1,13},{6,2},{10,6},{... | collective-permute-start | bytes 393224 | tf_op jit(solution)/shard_map/ppermute | solution.py:448
  22.1 1.3 %collective-permute-start.4 = (bf16[8,16,256]{2,1,0:T(8,128)(2,1)S(1)}, bf16[8,16,256]{2,1,0:T(8,128)(2,1)S(1)}, u32[]{:S(2)}, u32[]{:S(2)}) collective-permute-start(bf16[8,16,256]{2,1,0:T(8,128)(2,1)S(1)} %get-tuple-element.47), channel_id=1, source_target_pairs={{8,0},{9,1},{10,2},{11,3},{24,16},{25,17},{26,18},{27,19}} | collective-permute-start | bytes 196616 | tf_op jit(solution)/shard_map/ppermute | solution.py:448
  23.4 1.9 %values.2 = (bf16[512,1024]{1,0:T(8,128)(2,1)}, bf16[33,16,512]{2,1,0:T(8,128)(2,1)S(1)}, f32[2,128,2048]{2,1,0:T(8,128)S(1)}) custom-call(s32[4]{0:T(128)S(1)} %copy-done, s32[128]{0:T(128)S(1)} %copy-done.1, bf16[512,256]{1,0:T(8,128)(2,1)S(1)} %collective-permute-done.v_ref, bf16[512,256]{1,0:T(8,128)(2,1)S(1)} %collective-permute-done.1.k_ref, ...), custom_call_target="tpu_custom_call" | custom-call | flops 536870912 | bytes 3145728 | tf_op jit(solution)/shard_map/values/pallas_call | solution.py:453
  25.2 0.0 collective-permute-done.3.k_ref
  25.3 0.8 %scores.3 = (bf16[2,2,512,1024]{3,2,1,0:T(8,128)(2,1)S(1)}, f32[2,8,2048]{2,1,0:T(8,128)S(1)}, f32[2,8,2048]{2,1,0:T(8,128)S(1)}) custom-call(s32[4]{0:T(128)S(1)} %copy-done, bf16[512,1024]{1,0:T(8,128)(2,1)S(1)} %get-tuple-element.27.q_ref, bf16[512,256]{1,0:T(8,128)(2,1)S(1)} %collective-permute-done.3.k_ref, ...), custom_call_target="tpu_custom_call" | custom-call | flops 536870912 | bytes 3145728 | tf_op jit(solution)/shard_map/scores/pallas_call | solution.py:432
  26.0 1.4 %collective-permute-done.2.v_ref = bf16[512,256]{1,0:T(8,128)(2,1)S(1)} collective-permute-done((bf16[512,256]{1,0:T(8,128)(2,1)S(1)}, bf16[512,256]{1,0:T(8,128)(2,1)S(1)}, u32[]{:S(2)}, u32[]{:S(2)}) %collective-permute-start.2) | collective-permute-done | bytes 262176 | tf_op jit(solution)/shard_map/ppermute | solution.py:443
  27.5 1.7 %collective-permute-done.4.refs_1_ = bf16[8,16,256]{2,1,0:T(8,128)(2,1)S(1)} collective-permute-done((bf16[8,16,256]{2,1,0:T(8,128)(2,1)S(1)}, bf16[8,16,256]{2,1,0:T(8,128)(2,1)S(1)}, u32[]{:S(2)}, u32[]{:S(2)}) %collective-permute-start.4) | collective-permute-done | bytes 65568 | tf_op jit(solution)/shard_map/ppermute | solution.py:448
  29.1 0.0 collective-permute-done.5.refs_2_
  29.2 1.5 %values.3 = (bf16[512,1024]{1,0:T(8,128)(2,1)}, bf16[32,16,512]{2,1,0:T(8,128)(2,1)}) custom-call(s32[4]{0:T(128)S(1)} %copy-done, s32[27]{0:T(128)S(1)} %get-tuple-element.26.slot_ref, bf16[512,256]{1,0:T(8,128)(2,1)S(1)} %collective-permute-done.2.v_ref, bf16[512,256]{1,0:T(8,128)(2,1)S(1)} %collective-permute-done.3.k_ref, ...), custom_call_target="tpu_custom_call", output_to_operand_aliasing={{0}: (10, {})} | custom-call | flops 536870912 | bytes 3145728 | tf_op jit(solution)/shard_map/values/pallas_call | solution.py:453
Async XLA Ops:
  0.6 12.4 %collective-permute-start.1 = (bf16[512,256]{1,0:T(8,128)(2,1)}, bf16[512,256]{1,0:T(8,128)(2,1)S(1)}, u32[]{:S(2)}, u32[]{:S(2)}) collective-permute-start(bf16[512,256]{1,0:T(8,128)(2,1)} %k_hbm.1), channel_id=1, source_target_pairs={{0,4},{4,8},{8,12},{12,0},{1,5},{5,9},{9,13},{13,1},{2,6},{6,10},{... | collective-permute-start | bytes 786440 | tf_op jit(solution)/shard_map/ppermute | solution.py:396
  3.7 15.0 %collective-permute-start = (bf16[512,256]{1,0:T(8,128)(2,1)}, bf16[512,256]{1,0:T(8,128)(2,1)S(1)}, u32[]{:S(2)}, u32[]{:S(2)}) collective-permute-start(bf16[512,256]{1,0:T(8,128)(2,1)} %v_hbm.1), channel_id=1, source_target_pairs={{0,4},{4,8},{8,12},{12,0},{1,5},{5,9},{9,13},{13,1},{2,6},{6,10},{... | collective-permute-start | bytes 786440 | tf_op jit(solution)/shard_map/ppermute | solution.py:396
  5.3 0.7 %copy-start = (s32[4]{0:T(128)S(1)}, s32[4]{0:T(128)}, u32[]{:S(2)}) copy-start(s32[4]{0:T(128)} %lengths_ref.9) | copy-start | bytes 52
  5.9 0.7 %copy-start.1 = (s32[128]{0:T(128)S(1)}, s32[128]{0:T(128)}, u32[]{:S(2)}) copy-start(s32[128]{0:T(128)} %slot_ref.3) | copy-start | bytes 1540
  13.1 12.2 %collective-permute-start.3 = (bf16[512,256]{1,0:T(8,128)(2,1)S(1)}, bf16[512,256]{1,0:T(8,128)(2,1)S(1)}, u32[]{:S(2)}, u32[]{:S(2)}) collective-permute-start(bf16[512,256]{1,0:T(8,128)(2,1)S(1)} %collective-permute-done.1.k_ref), channel_id=1, source_target_pairs={{0,4},{4,8},{8,12},{12,0},{1,5},{5,9},{9,13},{13,1},{2,6},{6,10},{... | collective-permute-start | bytes 786440 | tf_op jit(solution)/shard_map/ppermute | solution.py:431
  18.7 8.8 %collective-permute-start.2 = (bf16[512,256]{1,0:T(8,128)(2,1)S(1)}, bf16[512,256]{1,0:T(8,128)(2,1)S(1)}, u32[]{:S(2)}, u32[]{:S(2)}) collective-permute-start(bf16[512,256]{1,0:T(8,128)(2,1)S(1)} %collective-permute-done.v_ref), channel_id=1, source_target_pairs={{0,4},{4,8},{8,12},{1,5},{5,9},{9,13},{2,6},{6,10},{10,14},{3,7},{... | collective-permute-start | bytes 786440 | tf_op jit(solution)/shard_map/ppermute | solution.py:443
  20.6 8.5 %collective-permute-start.5 = (bf16[8,16,512]{2,1,0:T(8,128)(2,1)S(1)}, bf16[8,16,512]{2,1,0:T(8,128)(2,1)S(1)}, u32[]{:S(2)}, u32[]{:S(2)}) collective-permute-start(bf16[8,16,512]{2,1,0:T(8,128)(2,1)S(1)} %get-tuple-element.49), channel_id=1, source_target_pairs={{4,0},{8,4},{12,8},{0,12},{5,1},{9,5},{13,9},{1,13},{6,2},{10,6},{... | collective-permute-start | bytes 393224 | tf_op jit(solution)/shard_map/ppermute | solution.py:448
  22.1 7.0 %collective-permute-start.4 = (bf16[8,16,256]{2,1,0:T(8,128)(2,1)S(1)}, bf16[8,16,256]{2,1,0:T(8,128)(2,1)S(1)}, u32[]{:S(2)}, u32[]{:S(2)}) collective-permute-start(bf16[8,16,256]{2,1,0:T(8,128)(2,1)S(1)} %get-tuple-element.47), channel_id=1, source_target_pairs={{8,0},{9,1},{10,2},{11,3},{24,16},{25,17},{26,18},{27,19}} | collective-permute-start | bytes 196616 | tf_op jit(solution)/shard_map/ppermute | solution.py:448
